TPU v7x, 256 devices: a whole 4x4x8 slice. The times are simulated.
256 devices in a mesh: dp: 128 (over z, y, x_lo, core), rep: 2 (over x_hi).
Axes of the slice: x: 4 (x_hi: 2, x_lo: 2; x = x_hi * 2 + x_lo), y: 4, z: 8, core: 2. Of those that a mesh axis runs over, the one named last changes fastest.
Arguments:
- picture_vectors: bfloat16 [65536, 1152], P('dp'), may hold values from -1 to 1
- caption_vectors: bfloat16 [65536, 1152], P('dp'), may hold values from -1 to 1
- matched_caption_index: int32 [128, 512], P('dp'), may hold values from 0 to 511, as said below
- score_multiplier: float32 [], replicated, may hold values from 90 to 110
- score_offset: float32 [], replicated, may hold values from -10.5 to -9.5
- objective_cotangent: float32 [], replicated, may hold values from 0.1 to 0.3
Outputs:
- picture_vector_derivative: float32 [65536, 1152], P('dp')
- caption_vector_derivative: float32 [65536, 1152], P('dp')
Inputs may be any that keep to these rules, and one draw needn't show every extreme that they name: Each row matched_caption_index[p] is a permutation of 0 .. 511.
All inputs are finite; a program needn't handle non-finite values.
Results may differ from a plain program's by a relative error of at most 0.0045.
Values may be sent and summed in bfloat16 or wider, within the bound.
A program may use at most 64 MiB of HBM per device.

v0:
```python
import jax
import jax.numpy as jnp
from jax import lax
from jax.sharding import PartitionSpec as P

STEPS = 8


def shifted(x, axis, by):
    devices = lax.axis_size(axis)
    return lax.ppermute(x, axis, [(i, (i + by) % devices) for i in range(devices)])


def per_device(
    picture_vectors,
    caption_vectors,
    matched_caption_index,
    score_multiplier,
    score_offset,
    objective_cotangent,
):
    rows = picture_vectors.shape[0]
    column = lax.broadcasted_iota(jnp.int32, (rows, rows), 1)
    match = (column == matched_caption_index.reshape(rows, 1)).astype(jnp.float32)
    replicas = lax.axis_size("rep")
    replica = lax.axis_index("rep")
    share = STEPS // replicas
    start_block = caption_vectors
    other = 1
    moved = shifted(caption_vectors, "dp", other * share)
    start_block = jnp.where(replica == other, moved, start_block)
    first_positive = jnp.where(replica == 0, 1.0, 0.0).astype(jnp.float32)
    text_block = start_block
    picture_derivative_piece = jnp.zeros(picture_vectors.shape, jnp.float32)
    caption_derivative_piece = jnp.zeros(text_block.shape, jnp.float32)
    for turn in range(share):
        if turn + 1 < share:
            following = shifted(text_block, "dp", 1)
        positive = first_positive if turn == 0 else 0.0
        block_picture_derivative_piece = picture_derivative_piece
        block_caption_derivative_piece = caption_derivative_piece
        inner_score_table = lax.dot_general(
            picture_vectors,
            text_block,
            (((1,), (1,)), ((), ())),
            preferred_element_type=jnp.float32,
        )
        couple_score_table = score_multiplier * inner_score_table + score_offset
        grads = (
            objective_cotangent * (jax.nn.sigmoid(couple_score_table) - positive * match)
        ).astype(jnp.bfloat16)
        block_picture_derivative_piece = block_picture_derivative_piece + jnp.dot(
            grads, text_block, preferred_element_type=jnp.float32
        )
        block_caption_derivative_piece = block_caption_derivative_piece + lax.dot_general(
            grads, picture_vectors, (((0,), (0,)), ((), ())), preferred_element_type=jnp.float32
        )
        picture_derivative_piece = block_picture_derivative_piece
        caption_derivative_piece = block_caption_derivative_piece
        if turn + 1 < share:
            caption_derivative_piece = shifted(caption_derivative_piece, "dp", 1)
            text_block = following
    picture_derivative_piece, caption_derivative_piece = (
        picture_derivative_piece,
        caption_derivative_piece,
    )
    caption_derivative_piece = shifted(caption_derivative_piece, "dp", -(share - 1))
    returned = caption_derivative_piece
    other = 1
    farther = shifted(caption_derivative_piece.astype(jnp.bfloat16), "dp", -(other * share)).astype(
        caption_derivative_piece.dtype
    )
    returned = jnp.where(replica == other, farther, returned)
    picture_derivative_piece, caption_derivative_piece = lax.psum(
        (picture_derivative_piece, returned), "rep"
    )
    return (
        score_multiplier * picture_derivative_piece,
        score_multiplier * caption_derivative_piece,
    )


def solution(mesh):
    placed = (P("dp", None), P("dp", None), P("dp", None), P(), P(), P())
    return jax.shard_map(
        per_device,
        mesh=mesh,
        in_specs=placed,
        out_specs=(P("dp", None), P("dp", None)),
        check_vma=False,
    )
```

profile of v0, /device:TPU:1, one launch (start us, length us, event | category | flops | bytes accessed | tf_op | source)
XLA Modules:
  0.0 399.9 jit_solution(16596022522039157687)
XLA Ops:
  7.2 2.2 collective-permute-start
  11.4 30.7 %collective-permute-done = bf16[512,1152]{1,0:T(8,128)(2,1)S(1)} collective-permute-done((bf16[512,1152]{1,0:T(8,128)(2,1)}, bf16[512,1152]{1,0:T(8,128)(2,1)S(1)}, u32[]{:S(2)}, u32[]{:S(2)}) %collective-permute-start) | collective-permute-done | bytes 1179680 | tf_op jit(solution)/shard_map/ppermute | solution.py:11
  42.1 1.4 broadcast_select_fusion
  43.5 1.1 fusion.26
  44.6 0.9 fusion.31
  45.5 2.4 collective-permute-start.4
  48.0 38.3 %collective-permute-done.1 = bf16[512,1152]{1,0:T(8,128)(2,1)S(1)} collective-permute-done((bf16[512,1152]{1,0:T(8,128)(2,1)S(1)}, bf16[512,1152]{1,0:T(8,128)(2,1)S(1)}, u32[]{:S(2)}, u32[]{:S(2)}) %collective-permute-start.1) | collective-permute-done | bytes 1179680 | tf_op jit(solution)/shard_map/ppermute | solution.py:11
  86.3 1.0 fusion.27
  87.3 0.9 convolution_add_fusion
  88.2 2.6 collective-permute-start.5
  90.9 38.3 %collective-permute-done.2 = bf16[512,1152]{1,0:T(8,128)(2,1)S(1)} collective-permute-done((bf16[512,1152]{1,0:T(8,128)(2,1)S(1)}, bf16[512,1152]{1,0:T(8,128)(2,1)S(1)}, u32[]{:S(2)}, u32[]{:S(2)}) %collective-permute-start.2) | collective-permute-done | bytes 1179680 | tf_op jit(solution)/shard_map/ppermute | solution.py:11
  129.2 1.0 fusion.28
  130.2 0.9 fusion.32
  131.2 0.2 add.69
  131.4 2.6 collective-permute-start.6
  134.0 0.1 collective-permute-start.3
  134.0 38.3 %collective-permute-done.3 = bf16[512,1152]{1,0:T(8,128)(2,1)S(1)} collective-permute-done((bf16[512,1152]{1,0:T(8,128)(2,1)S(1)}, bf16[512,1152]{1,0:T(8,128)(2,1)S(1)}, u32[]{:S(2)}, u32[]{:S(2)}) %collective-permute-start.3) | collective-permute-done | bytes 1179680 | tf_op jit(solution)/shard_map/ppermute | solution.py:11
  172.4 1.0 fusion.29
  173.4 0.9 fusion.33
  174.3 0.2 add.70
  174.6 3.9 collective-permute-start.7
  178.5 40.3 %collective-permute-done.7 = f32[512,1152]{1,0:T(8,128)S(1)} collective-permute-done((f32[512,1152]{1,0:T(8,128)S(1)}, f32[512,1152]{1,0:T(8,128)S(1)}, u32[]{:S(2)}, u32[]{:S(2)}) %collective-permute-start.7) | collective-permute-done | bytes 2359328 | tf_op jit(solution)/shard_map/ppermute | solution.py:11
  218.8 0.1 convert_element_type.23
  219.0 16.0 %collective-permute-start.8 = (bf16[512,1152]{1,0:T(8,128)(2,1)S(1)}, bf16[512,1152]{1,0:T(8,128)(2,1)S(1)}, u32[]{:S(2)}, u32[]{:S(2)}) collective-permute-start(bf16[512,1152]{1,0:T(8,128)(2,1)S(1)} %convert_element_type.23), channel_id=1, source_target_pairs={{0,248},{2,250},{4,252},{6,254},{8,0},{10,2},{12,4},{14,6},{16,8},... | collective-permute-start | bytes 3538952 | tf_op jit(solution)/shard_map/ppermute | solution.py:11
  235.0 0.8 fusion.30
  235.8 0.9 convolution_add_fusion.3
  236.7 0.9 convolution_add_fusion.2
  237.6 2.3 convolution_add_fusion.1
  239.9 16.3 %collective-permute-done.8 = bf16[512,1152]{1,0:T(8,128)(2,1)S(1)} collective-permute-done((bf16[512,1152]{1,0:T(8,128)(2,1)S(1)}, bf16[512,1152]{1,0:T(8,128)(2,1)S(1)}, u32[]{:S(2)}, u32[]{:S(2)}) %collective-permute-start.8) | collective-permute-done | bytes 1179680 | tf_op jit(solution)/shard_map/ppermute | solution.py:11
  256.1 1.7 convert_select_fusion
  257.9 130.3 %all-reduce.3.cloned.1.call-done = (f32[512,1152]{1,0:T(8,128)}, f32[512,1152]{1,0:T(8,128)}) async-done(((f32[512,1152]{1,0:T(8,128)}, f32[512,1152]{1,0:T(8,128)}), (f32[512,1152]{1,0:T(8,128)}, f32[512,1152]{1,0:T(8,128)})) %all-reduce.3.cloned.1.call-update) | async-done | bytes 4718608 | tf_op jit(solution)/shard_map/psum | solution.py:74
  388.2 4.9 %broadcast_multiply_fusion = (f32[512,1152]{1,0:T(8,128)}, f32[512,1152]{1,0:T(8,128)}) fusion(f32[512,1152]{1,0:T(8,128)} %get-tuple-element.3, f32[]{:T(128)S(6)} %copy.21, f32[512,1152]{1,0:T(8,128)} %get-tuple-element.2), kind=kLoop, calls=%fused_computation.39 | loop fusion | flops 1179648 | bytes 9437188 | tf_op jit(solution)/shard_map/mul | solution.py:79
  (11 shorter events, 0.3 us)
Async XLA Ops:
  7.2 36.3 %copy-start = (bf16[512,1152]{1,0:T(8,128)(2,1)S(1)}, bf16[512,1152]{1,0:T(8,128)(2,1)}, u32[]{:S(2)}) copy-start(bf16[512,1152]{1,0:T(8,128)(2,1)} %param.6) | copy-start | bytes 3538948
  7.2 381.0 %all-reduce.3.cloned.1.call-start = ((), (), s32[]{:S(2)}) async-start(), calls=%async_computation | async-start | bytes 9437184 | tf_op jit(solution)/shard_map/psum | solution.py:74
  7.2 34.8 %collective-permute-start = (bf16[512,1152]{1,0:T(8,128)(2,1)}, bf16[512,1152]{1,0:T(8,128)(2,1)S(1)}, u32[]{:S(2)}, u32[]{:S(2)}) collective-permute-start(bf16[512,1152]{1,0:T(8,128)(2,1)} %param.7), channel_id=1, source_target_pairs={{0,8},{2,10},{4,12},{6,14},{8,16},{10,18},{12,20},{14,22},{16,24},... | collective-permute-start | bytes 3538952 | tf_op jit(solution)/shard_map/ppermute | solution.py:11
  11.4 32.1 %copy-start.1 = (s32[1,512]{1,0:T(1,128)S(1)}, s32[1,512]{1,0:T(1,128)}, u32[]{:S(2)}) copy-start(s32[1,512]{1,0:T(1,128)} %param.8) | copy-start | bytes 6148
  45.5 41.9 %collective-permute-start.4 = (f32[512,1152]{1,0:T(8,128)S(1)}, f32[512,1152]{1,0:T(8,128)S(1)}, u32[]{:S(2)}, u32[]{:S(2)}) collective-permute-start(f32[512,1152]{1,0:T(8,128)S(1)} %fusion.31), channel_id=1, source_target_pairs={{0,2},{2,4},{4,6},{6,8},{8,10},{10,12},{12,14},{14,16},{16,18},{18... | collective-permute-start | bytes 7077896 | tf_op jit(solution)/shard_map/ppermute | solution.py:11
  47.9 38.4 %collective-permute-start.1 = (bf16[512,1152]{1,0:T(8,128)(2,1)S(1)}, bf16[512,1152]{1,0:T(8,128)(2,1)S(1)}, u32[]{:S(2)}, u32[]{:S(2)}) collective-permute-start(bf16[512,1152]{1,0:T(8,128)(2,1)S(1)} %broadcast_select_fusion), channel_id=1, source_target_pairs={{0,2},{2,4},{4,6},{6,8},{8,10},{10,12},{12,14},{14,16},{16,18},{18... | collective-permute-start | bytes 3538952 | tf_op jit(solution)/shard_map/ppermute | solution.py:11
  88.2 42.9 %collective-permute-start.5 = (f32[512,1152]{1,0:T(8,128)S(1)}, f32[512,1152]{1,0:T(8,128)S(1)}, u32[]{:S(2)}, u32[]{:S(2)}) collective-permute-start(f32[512,1152]{1,0:T(8,128)S(1)} %convolution_add_fusion), channel_id=1, source_target_pairs={{0,2},{2,4},{4,6},{6,8},{8,10},{10,12},{12,14},{14,16},{16,18},{18... | collective-permute-start | bytes 7077896 | tf_op jit(solution)/shard_map/ppermute | solution.py:11
  90.8 38.4 %collective-permute-start.2 = (bf16[512,1152]{1,0:T(8,128)(2,1)S(1)}, bf16[512,1152]{1,0:T(8,128)(2,1)S(1)}, u32[]{:S(2)}, u32[]{:S(2)}) collective-permute-start(bf16[512,1152]{1,0:T(8,128)(2,1)S(1)} %collective-permute-done.1), channel_id=1, source_target_pairs={{0,2},{2,4},{4,6},{6,8},{8,10},{10,12},{12,14},{14,16},{16,18},{18... | collective-permute-start | bytes 3538952 | tf_op jit(solution)/shard_map/ppermute | solution.py:11
  131.4 42.9 %collective-permute-start.6 = (f32[512,1152]{1,0:T(8,128)S(1)}, f32[512,1152]{1,0:T(8,128)S(1)}, u32[]{:S(2)}, u32[]{:S(2)}) collective-permute-start(f32[512,1152]{1,0:T(8,128)S(1)} %add.69), channel_id=1, source_target_pairs={{0,2},{2,4},{4,6},{6,8},{8,10},{10,12},{12,14},{14,16},{16,18},{18... | collective-permute-start | bytes 7077896 | tf_op jit(solution)/shard_map/ppermute | solution.py:11
  134.0 38.4 %collective-permute-start.3 = (bf16[512,1152]{1,0:T(8,128)(2,1)S(1)}, bf16[512,1152]{1,0:T(8,128)(2,1)S(1)}, u32[]{:S(2)}, u32[]{:S(2)}) collective-permute-start(bf16[512,1152]{1,0:T(8,128)(2,1)S(1)} %collective-permute-done.2), channel_id=1, source_target_pairs={{0,2},{2,4},{4,6},{6,8},{8,10},{10,12},{12,14},{14,16},{16,18},{18... | collective-permute-start | bytes 3538952 | tf_op jit(solution)/shard_map/ppermute | solution.py:11
  174.6 44.3 %collective-permute-start.7 = (f32[512,1152]{1,0:T(8,128)S(1)}, f32[512,1152]{1,0:T(8,128)S(1)}, u32[]{:S(2)}, u32[]{:S(2)}) collective-permute-start(f32[512,1152]{1,0:T(8,128)S(1)} %add.70), channel_id=1, source_target_pairs={{0,250},{2,252},{4,254},{6,0},{8,2},{10,4},{12,6},{14,8},{16,10},{... | collective-permute-start | bytes 7077896 | tf_op jit(solution)/shard_map/ppermute | solution.py:11
  219.0 37.2 %collective-permute-start.8 = (bf16[512,1152]{1,0:T(8,128)(2,1)S(1)}, bf16[512,1152]{1,0:T(8,128)(2,1)S(1)}, u32[]{:S(2)}, u32[]{:S(2)}) collective-permute-start(bf16[512,1152]{1,0:T(8,128)(2,1)S(1)} %convert_element_type.23), channel_id=1, source_target_pairs={{0,248},{2,250},{4,252},{6,254},{8,0},{10,2},{12,4},{14,6},{16,8},... | collective-permute-start | bytes 3538952 | tf_op jit(solution)/shard_map/ppermute | solution.py:11
Sparse Core Ops, SparseCore 0:
  258.0 130.1 all-reduce.2
where the time goes:
time: 400 us
  waiting for transfers between devices  333 us (83%)
  starting transfers between devices  30 us (8%)
  between operations  16.1 us (4%)
  matrix products  12.5 us (3%)
  other arithmetic  8.55 us (2%)
    ppermute x9, waiting for transfers between devices, shifted(): lax.ppermute(x, axis, [(i, (i + by) % devices) for i in range(devices)])  202 us
    psum x1, waiting for transfers between devices, per_device(): lax.psum((picture_derivative_piece, returned), 'rep')  130 us
    ppermute x9, starting transfers between devices, shifted(): lax.ppermute(x, axis, [(i, (i + by) % devices) for i in range(devices)])  30 us
  transfers between devices with their start and end apart: 10, of which 7 were waited for; matrix products, arithmetic and copies ran while one was open for 2% of the time, Pallas kernels for 0%

commit v1 on v0

v1 whole, which is shorter than its diff:
```python
import functools

import jax
import jax.numpy as jnp
from jax import lax
from jax.experimental import pallas as pl
from jax.experimental.pallas import tpu as pltpu
from jax.sharding import PartitionSpec as P

MESH = pl.DeviceIdType.MESH
PIECES = 4

NAMES = (
    "sib", "b1_0", "b1_1", "a2_0", "a2_1", "b2_0", "b2_1", "a1_0", "a1_1",
    "b3_0", "b3_1", "a3_0", "a3_1", "a4", "b4",
)
SLOT = {name: i for i, name in enumerate(NAMES)}

FORWARD = (
    {
        "a2_0": lambda j: [("X", "b3_1"), ("S", "a2_0")] if j < 2 else [("S", "a2_0")],
        "b1_0": lambda j: [("S", "b1_0")],
        "b2_0": lambda j: [("X", "a1_1"), ("P", "b4"), ("S", "b2_0")],
        "a1_0": lambda j: [("N", "a3_0"), ("S", "a1_0")],
        "b3_0": lambda j: [("S", "b3_0")],
        "b4": lambda j: [("X", "a3_1"), ("S", "b4")],
        "a3_0": lambda j: [("S", "a3_0")],
    },
    {
        "a2_1": lambda j: [("X", "b3_0"), ("N0", "a4"), ("S", "a2_1")],
        "b1_1": lambda j: [("P", "b3_1"), ("S", "b1_1")] if j >= 2 else [("S", "b1_1")],
        "b2_1": lambda j: [("X", "a1_0"), ("S", "b2_1")],
        "a1_1": lambda j: [("S", "a1_1")],
        "b3_1": lambda j: [("X", "a2_0"), ("S", "b3_1")] if j >= 2 else [("S", "b3_1")],
        "a3_1": lambda j: [("S", "a3_1")],
    },
)

PLAN = (
    [
        "b2_0:0", "a2_0:0", "b1_0:0", "b1_0:1", "b2_0:1", "a2_0:1", "b1_0:2", "b1_0:3", "T.b1_0",
        "T.b1_1",
        "b2_0:2", "a1_0:0", "a1_0:1", "T.a2_1",
        "b2_0:3", "T.b2_0",
        "b3_0:0", "b3_0:1", "T.b2_1",
        "a1_0:2", "b4:0", "a1_0:3", "T.a1_0",
        "b3_0:2", "b3_0:3", "T.b3_0",
        "b4:1", "T.a1_1",
        "a3_0:0", "b4:2", "T.a4",
        "a3_0:1", "a2_0:2", "a2_0:3", "T.b3_1",
        "T.a2_0",
        "b4:3", "a3_0:2", "H.a3_0.0",
        "a3_0:3", "H.a3_0.1",
        "H.a3_1.0",
        "H.a3_1.1",
    ],
    [
        "b2_1:0", "a2_1:0", "b1_1:0", "b1_1:1", "b2_1:1", "a2_1:1", "b1_1:2", "b1_1:3", "T.b1_1",
        "T.b1_0",
        "a2_1:2", "b2_1:2", "a2_1:3", "T.a2_1",
        "a1_1:0", "a1_1:1", "b2_1:3", "T.b2_1",
        "b3_1:0", "b3_1:1", "T.b2_0",
        "b3_1:2", "a1_1:2", "a1_1:3", "T.a1_1",
        "b3_1:3", "T.b3_0",
        "T.a1_0",
        "T.b3_1",
        "T.a2_0",
        "a3_1:0", "a3_1:1", "T.b4",
        "H.a3_0.0",
        "a3_1:2", "a3_1:3", "H.a3_0.1",
        "H.a3_1.0",
        "H.a3_1.1",
    ],
)


def coordinates():
    shard, replica = lax.axis_index("dp"), lax.axis_index("rep")
    return shard // 16, (shard // 4) % 4, replica * 2 + (shard // 2) % 2, shard % 2


def device(z, y, x, core):
    return (z * 16 + y * 4 + (x % 2) * 2 + core, x // 2)


def kernel(
    rows, scalars, match_ref, picture_hbm, caption_hbm, picture_out, caption_out,
    own, held, total, load_sem, send_sem, recv_sem, store_sem,
):
    z, y, x, core = coordinates()
    kind = x % 2
    logical = (core + kind) % 2
    part = rows // PIECES
    up = ((z + (y + 1) // 4) % 8, (y + 1) % 4)
    down = ((z + 7 + (y + 3) // 4) % 8, (y + 3) % 4)
    next_z, next_y = [u * (1 - kind) + d * kind for u, d in zip(up, down)]
    prev_z, prev_y = [d * (1 - kind) + u * kind for u, d in zip(up, down)]
    place = {
        "S": device(z, y, x, 1 - core),
        "N": device(next_z, next_y, x, core),
        "P": device(prev_z, prev_y, x, core),
        "N0": device(next_z, next_y, x, kind),
        "P1": device(prev_z, prev_y, x, 1 - kind),
        "R": device(z, y, (x + 1) % 4, core),
        "L": device(z, y, (x + 3) % 4, core),
    }

    loads = [
        pltpu.make_async_copy(picture_hbm, own.at[1 - kind], load_sem.at[0]),
        pltpu.make_async_copy(caption_hbm, own.at[kind], load_sem.at[1]),
    ]
    for load in loads:
        load.start()

    barrier = pltpu.get_barrier_semaphore()
    for where in "SNPRL":
        pl.semaphore_signal(barrier, inc=1, device_id=place[where], device_id_type=MESH)

    @pl.when(logical == 0)
    def _():
        pl.semaphore_signal(barrier, inc=1, device_id=place["P1"], device_id_type=MESH)
        pl.semaphore_wait(barrier, 5)

    @pl.when(logical == 1)
    def _():
        pl.semaphore_wait(barrier, 6)

    for load in loads:
        load.wait()

    sent = ([], [])

    def piece(ref, block, j, count=1):
        return ref.at[block, pl.ds(j * part, count * part)]

    def send(c, src, where, name, j, count=1):
        if where == "X":
            where = "RL"[j % 2]
        index = len(sent[c])

        def copy():
            return pltpu.make_async_remote_copy(
                src_ref=piece(src[0], src[1], j, count),
                dst_ref=piece(held, SLOT[name], j, count),
                send_sem=send_sem.at[index],
                recv_sem=recv_sem.at[SLOT[name], j],
                device_id=place[where],
                device_id_type=MESH,
            )

        copy().start()
        sent[c].append(copy)

    def arrived(name, j, count=1):
        here = piece(held, SLOT[name], j, count)
        pltpu.make_async_remote_copy(
            src_ref=here, dst_ref=here, send_sem=send_sem.at[0], recv_sem=recv_sem.at[SLOT[name], j],
            device_id=place["S"], device_id_type=MESH,
        ).wait_recv()

    for c in (0, 1):

        @pl.when(logical == c)
        def _(c=c):
            send(c, (own, c), "S", "sib", 0, PIECES)
            for j in range(PIECES):
                if c == 1 or j < 2:
                    send(c, (own, 0), "N", "a2_%d" % c, j)
                send(c, (own, 1), "P", "b2_%d" % c, j)
                send(c, (own, 0), "X", "b1_%d" % (1 - c), j)

    multiplier, offset, cotangent = scalars[0], scalars[1], scalars[2]
    slope, shift = -multiplier, -offset

    def gradient(left, right):
        table = lax.dot_general(left, right, (((1,), (1,)), ((), ())), preferred_element_type=jnp.float32)
        return cotangent / (1.0 + jnp.exp(slope * table + shift))

    row = lax.broadcasted_iota(jnp.int32, (rows, rows), 0)
    paired = (row == match_ref[...]).astype(jnp.float32)
    turned = paired.T
    is_a = (kind == 0).astype(jnp.float32)
    positive = is_a * turned + (1.0 - is_a) * paired
    first = (gradient(own[1], own[0]) - cotangent * positive).astype(jnp.bfloat16)
    total[0] = jnp.dot(first, own[0], preferred_element_type=jnp.float32)
    total[1] = lax.dot_general(first, own[1], (((0,), (0,)), ((), ())), preferred_element_type=jnp.float32)

    half = rows // 2

    def work(which, block, start, size):
        @pl.loop(0, rows, step=half)
        def _(r):
            here = pl.ds(pl.multiple_of(r, half), half)
            other = held[block, pl.ds(start, size)]
            grads = gradient(own[1 - which, here], other).astype(jnp.bfloat16)
            total[which, here] += jnp.dot(grads, other, preferred_element_type=jnp.float32)

    def pick(values):
        return values[0] if values[0] == values[1] else values[0] * (1 - logical) + values[1] * logical

    arrived("sib", 0, PIECES)
    work(1 - logical, SLOT["sib"], 0, rows)

    position = [0, 0]
    waited = [set(), set()]
    while position[0] < len(PLAN[0]):
        step = []
        for c in (0, 1):
            events = []
            while PLAN[c][position[c]][1] != ".":
                events.append(PLAN[c][position[c]])
                position[c] += 1
            task = PLAN[c][position[c]].split(".")
            position[c] += 1
            step.append(task)

            @pl.when(logical == c)
            def _(c=c, events=events, task=task):
                for event in events:
                    name, j = event.split(":")
                    j = int(j)
                    arrived(name, j)
                    waited[c].add((name, j))
                    for where, target in FORWARD[c][name](j):
                        send(c, (held, SLOT[name]), where, target, j)
                pieces = range(PIECES) if task[0] == "T" else range(2 * int(task[2]), 2 * int(task[2]) + 2)
                for j in pieces:
                    if (task[1], j) not in waited[c]:
                        assert task[1] not in FORWARD[c]
                        arrived(task[1], j)
                        waited[c].add((task[1], j))

        block = pick([SLOT[task[1]] for task in step])
        which = pick([0 if task[1][0] == "a" else 1 for task in step])
        if step[0][0] == "T":
            work(which, block, 0, rows)
        else:
            work(which, block, half * int(step[0][2]), half)

    for c in (0, 1):

        @pl.when(logical == c)
        def _(c=c):
            for name in NAMES:
                for j in range(PIECES):
                    assert (name, j) in waited[c] or name in ("sib", "a4" if c else "")
            for copy in sent[c]:
                copy().wait_send()

    total[...] = total[...] * multiplier
    for value in (0, 1):

        @pl.when(kind == value)
        def _(value=value):
            stores = [
                pltpu.make_async_copy(total.at[value], picture_out, store_sem.at[0]),
                pltpu.make_async_copy(total.at[1 - value], caption_out, store_sem.at[1]),
            ]
            for store in stores:
                store.start()
            for store in stores:
                store.wait()


def per_device(pictures, captions, matched, multiplier, offset, cotangent):
    rows, width = pictures.shape
    scalars = jnp.stack([multiplier, offset, cotangent])
    out = jax.ShapeDtypeStruct((rows, width), jnp.float32)
    return pl.pallas_call(
        functools.partial(kernel, rows),
        out_shape=(out, out),
        in_specs=[
            pl.BlockSpec(memory_space=pltpu.SMEM),
            pl.BlockSpec(memory_space=pltpu.VMEM),
            pl.BlockSpec(memory_space=pl.ANY),
            pl.BlockSpec(memory_space=pl.ANY),
        ],
        out_specs=(pl.BlockSpec(memory_space=pl.ANY), pl.BlockSpec(memory_space=pl.ANY)),
        scratch_shapes=[
            pltpu.VMEM((2, rows, width), jnp.bfloat16),
            pltpu.VMEM((len(NAMES), rows, width), jnp.bfloat16),
            pltpu.VMEM((2, rows, width), jnp.float32),
            pltpu.SemaphoreType.DMA((2,)),
            pltpu.SemaphoreType.DMA((80,)),
            pltpu.SemaphoreType.DMA((len(NAMES), PIECES)),
            pltpu.SemaphoreType.DMA((2,)),
        ],
        compiler_params=pltpu.CompilerParams(
            collective_id=0, has_side_effects=True, vmem_limit_bytes=52 * 2**20
        ),
        cost_estimate=pl.CostEstimate(
            flops=31 * 2 * rows * rows * width, bytes_accessed=12 * rows * width, transcendentals=16 * rows * rows
        ),
        name="band",
    )(scalars, matched, pictures, captions)


def solution(mesh):
    placed = (P("dp", None), P("dp", None), P("dp", None), P(), P(), P())
    return jax.shard_map(
        per_device,
        mesh=mesh,
        in_specs=placed,
        out_specs=(P("dp", None), P("dp", None)),
        check_vma=False,
    )
```

time: 400 us -> 88.6 us (0.22)
  waiting for transfers between devices: 333 us -> 0 us
  Pallas kernels: 0 us -> 79 us
  starting transfers between devices: 30 us -> 0 us
  between operations: 16.1 us -> 2.59 us
  matrix products: 12.5 us -> 0 us
  other arithmetic: 8.55 us -> 0.08 us
  local copies, waits for them, and re-layouts: 0.01 us -> 6.74 us
    ppermute x9 -> x0, waiting for transfers between devices: 202 us -> none  [shifted(): lax.ppermute(x, axis, [(i, (i + by) % devices) for i in range(devices)])]
    psum x1 -> x0, waiting for transfers between devices: 130 us -> none  [per_device(): lax.psum((picture_derivative_piece, returned), 'rep')]
    pallas_call x0 -> x1, Pallas kernels: none -> 79 us  [per_device(): pl.pallas_call(functools.partial(kernel, rows), out_shape=(out, out), in_...]
    ppermute x9 -> x0, starting transfers between devices: 30 us -> none  [shifted(): lax.ppermute(x, axis, [(i, (i + by) % devices) for i in range(devices)])]
    dot_general x12 -> x0, matrix products: 12.5 us -> none  [the longest x4 4.84 us: per_device(): jnp.dot(grads, text_block, preferred_element_type=jnp.float32)]
    unnamed x4 -> x8, local copies, waits for them, and re-layouts: 0.01 us -> 6.74 us
    mul x1 -> x0, other arithmetic: 4.86 us -> none  [per_device(): score_multiplier * caption_derivative_piece]
  transfers between devices with their start and end apart: 10 -> 0, of which waited for: 7 -> 0; matrix products, arithmetic and copies ran while one was open for 2% -> 0% of each run, Pallas kernels for 0% -> 0%
where the time goes in v1:
time: 88.6 us; the launch traced here: 88.4 us
  Pallas kernels  79 us (89%)
  local copies, waits for them, and re-layouts  6.74 us (8%)
  between operations  2.59 us (3%)
    pallas_call x1, Pallas kernels, per_device(): pl.pallas_call(functools.partial(kernel, rows), out_shape=(out, out), in_...  79 us
    unnamed x8, local copies, waits for them, and re-layouts  6.74 us

profile of v1, /device:TPU:1, one launch (start us, length us, event | category | flops | bytes accessed | tf_op | source)
XLA Modules:
  0.0 88.4 jit_solution(9814512880365770528)
XLA Ops:
  2.6 0.1 pad_maximum_fusion.scalars
  2.6 0.0 copy-start
  2.6 1.3 %copy-done = bf16[512,1152]{1,0:T(8,128)(2,1)S(1)} copy-done((bf16[512,1152]{1,0:T(8,128)(2,1)S(1)}, bf16[512,1152]{1,0:T(8,128)(2,1)}, u32[]{:S(2)}) %copy-start) | copy-done | bytes 1179672
  3.9 0.0 copy-start.1
  3.9 0.7 copy-done.1
  4.6 79.0 %band.1 = (f32[512,1152]{1,0:T(8,128)}, f32[512,1152]{1,0:T(8,128)}) custom-call(f32[3]{0:T(128)S(1)} %pad_maximum_fusion.scalars, s32[1,512]{1,0:T(1,128)S(1)} %copy-done.1, bf16[512,1152]{1,0:T(8,128)(2,1)S(1)} %copy-done, bf16[512,1152]{1,0:T(8,128)(2,1)} %caption_hbm.1), custom_call_target="tpu_custom_call" | custom-call | flops 18723373056 | bytes 7077888 | tf_op jit(solution)/shard_map/band/pallas_call | solution.py:269
  83.6 0.0 copy-start.2
  83.6 3.4 %copy.13 = f32[512,1152]{1,0:T(8,128)} copy(f32[512,1152]{1,0:T(8,128)} %get-tuple-element.4) | data formatting | bytes 4718592
  87.0 0.0 copy-done.2
  87.0 1.4 %copy.14 = f32[512,1152]{1,0:T(8,128)} copy(f32[512,1152]{1,0:T(8,128)S(1)} %copy-done.2) | data formatting | bytes 4718592
Async XLA Ops:
  2.6 1.3 %copy-start = (bf16[512,1152]{1,0:T(8,128)(2,1)S(1)}, bf16[512,1152]{1,0:T(8,128)(2,1)}, u32[]{:S(2)}) copy-start(bf16[512,1152]{1,0:T(8,128)(2,1)} %picture_hbm.1) | copy-start | bytes 3538948
  3.9 0.7 copy-start.1
  83.6 3.4 %copy-start.2 = (f32[512,1152]{1,0:T(8,128)S(1)}, f32[512,1152]{1,0:T(8,128)}, u32[]{:S(2)}) copy-start(f32[512,1152]{1,0:T(8,128)} %get-tuple-element.5) | copy-start | bytes 7077892

commit v2 on v1

v2 whole, which is shorter than its diff:
```python
import functools

import jax
import jax.numpy as jnp
from jax import lax
from jax.experimental import pallas as pl
from jax.experimental.pallas import tpu as pltpu
from jax.sharding import PartitionSpec as P

MESH = pl.DeviceIdType.MESH
PIECES = 4
SPLIT = 3
LIMIT = 36

NAMES = (
    "sib", "b1_0", "b1_1", "a2_0", "a2_1", "b2_0", "b2_1", "a1_0", "a1_1",
    "b3_0", "b3_1", "a3_0", "a3_1", "a4", "b4",
)
SLOT = {name: i for i, name in enumerate(NAMES)}

FORWARD = (
    {
        "a2_0": lambda j: [("X", "b3_1"), ("S", "a2_0")] if j < SPLIT else [("S", "a2_0")],
        "b1_0": lambda j: [("S", "b1_0")],
        "b2_0": lambda j: [("X", "a1_1"), ("P", "b4"), ("S", "b2_0")],
        "a1_0": lambda j: [("N", "a3_0"), ("S", "a1_0")],
        "b3_0": lambda j: [("S", "b3_0")],
        "b4": lambda j: [("X", "a3_1"), ("S", "b4")],
        "a3_0": lambda j: [("S", "a3_0")],
    },
    {
        "a2_1": lambda j: [("X", "b3_0"), ("N0", "a4"), ("S", "a2_1")],
        "b1_1": lambda j: [("P", "b3_1"), ("S", "b1_1")] if j >= SPLIT else [("S", "b1_1")],
        "b2_1": lambda j: [("X", "a1_0"), ("S", "b2_1")],
        "a1_1": lambda j: [("S", "a1_1")],
        "b3_1": lambda j: [("X", "a2_0"), ("S", "b3_1")] if j >= SPLIT else [("S", "b3_1")],
        "a3_1": lambda j: [("S", "a3_1")],
    },
)

OWN = (
    [
        "P.b2_0:0", "X.b1_1:3", "P.b2_0:1", "X.b1_1:0", "N.a2_0:1", "P.b2_0:2", "N.a2_0:2", "X.b1_1:2",
        "N.a2_0:0", "X.b1_1:1", "P.b2_0:3",
    ],
    [
        "N.a2_1:2", "P.b2_1:3", "X.b1_0:0", "P.b2_1:2", "P.b2_1:0", "N.a2_1:3", "P.b2_1:1", "X.b1_0:3",
        "N.a2_1:1", "X.b1_0:2", "X.b1_0:1", "N.a2_1:0",
    ],
)

PLAN = (
    [
        "b2_0:0", "a2_0:1", "a2_0:2", "b2_0:1", "H.b1_1.1",
        "H.b1_1.0",
        "b2_0:2", "a2_0:0", "a1_0:3", "b1_0:3", "b1_0:1", "b1_0:0", "b1_0:2", "T.b1_0",
        "b2_0:3", "H.a2_0.0",
        "b3_0:2", "H.b2_1.1",
        "H.a2_1.1",
        "b3_0:3", "H.b3_0.1",
        "H.a2_1.0",
        "a1_0:2", "T.b2_0",
        "b3_0:1", "b4:0", "T.b3_1",
        "b4:1", "a1_0:1", "a1_0:0", "H.b2_1.0",
        "b4:2", "T.a1_0",
        "a3_0:3", "a2_0:3", "a3_0:2", "b4:3", "b3_0:0", "T.a1_1",
        "T.a4",
        "H.b3_0.0",
        "H.a2_0.1",
        "a3_0:1", "a3_0:0", "T.a3_0",
        "T.a3_1",
    ],
    [
        "b1_1:0", "b1_1:3", "b1_1:2", "b2_1:3", "a1_1:0", "b1_1:1", "a2_1:2", "H.b1_1.0",
        "a2_1:3", "H.a2_0.0",
        "b3_1:2", "b3_1:1", "a2_1:1", "H.b1_1.1",
        "b2_1:1", "b2_1:2", "a2_1:0", "T.a2_1",
        "b2_1:0", "T.b2_0",
        "b3_1:0", "b3_1:3", "T.b3_1",
        "a1_1:3", "T.b2_1",
        "T.b1_0",
        "a1_1:1", "H.a1_1.0",
        "a1_1:2", "H.a1_1.1",
        "T.a1_0",
        "H.a2_0.1",
        "T.b4",
        "a3_1:0", "T.b3_0",
        "a3_1:2", "a3_1:1", "a3_1:3", "T.a3_1",
        "T.a3_0",
    ],
)


def coordinates():
    shard, replica = lax.axis_index("dp"), lax.axis_index("rep")
    return shard // 16, (shard // 4) % 4, replica * 2 + (shard // 2) % 2, shard % 2


def device(z, y, x, core):
    return (z * 16 + y * 4 + (x % 2) * 2 + core, x // 2)


def kernel(
    rows, scalars, match_hbm, picture_hbm, caption_hbm, total,
    own, held, match_ref, load_sem, send_sem, recv_sem,
):
    z, y, x, core = coordinates()
    kind = x % 2
    logical = (core + kind) % 2
    part = rows // PIECES
    up = ((z + (y + 1) // 4) % 8, (y + 1) % 4)
    down = ((z + 7 + (y + 3) // 4) % 8, (y + 3) % 4)
    next_z, next_y = [u * (1 - kind) + d * kind for u, d in zip(up, down)]
    prev_z, prev_y = [d * (1 - kind) + u * kind for u, d in zip(up, down)]
    place = {
        "S": device(z, y, x, 1 - core),
        "N": device(next_z, next_y, x, core),
        "P": device(prev_z, prev_y, x, core),
        "N0": device(next_z, next_y, x, kind),
        "P1": device(prev_z, prev_y, x, 1 - kind),
        "R": device(z, y, (x + 1) % 4, core),
        "L": device(z, y, (x + 3) % 4, core),
    }

    loads = [
        pltpu.make_async_copy(picture_hbm, own.at[1 - kind], load_sem.at[0]),
        pltpu.make_async_copy(caption_hbm, own.at[kind], load_sem.at[1]),
        pltpu.make_async_copy(match_hbm, match_ref, load_sem.at[2]),
    ]
    for load in loads:
        load.start()

    barrier = pltpu.get_barrier_semaphore()
    for where in "SNPRL":
        pl.semaphore_signal(barrier, inc=1, device_id=place[where], device_id_type=MESH)

    @pl.when(logical == 0)
    def _():
        pl.semaphore_signal(barrier, inc=1, device_id=place["P1"], device_id_type=MESH)
        pl.semaphore_wait(barrier, 5)

    @pl.when(logical == 1)
    def _():
        pl.semaphore_wait(barrier, 6)

    for load in loads:
        load.wait()

    sent = ([], [])

    def piece(ref, block, j, count=1):
        return ref.at[block, pl.ds(j * part, count * part)]

    def send(c, src, where, name, j, count=1):
        if where == "X":
            where = "RL"[j % 2]
        index = len(sent[c])

        def copy():
            return pltpu.make_async_remote_copy(
                src_ref=piece(src[0], src[1], j, count),
                dst_ref=piece(held, SLOT[name], j, count),
                send_sem=send_sem.at[index],
                recv_sem=recv_sem.at[SLOT[name], j],
                device_id=place[where],
                device_id_type=MESH,
            )

        copy().start()
        sent[c].append(copy)

    def arrived(name, j, count=1):
        here = piece(held, SLOT[name], j, count)
        pltpu.make_async_remote_copy(
            src_ref=here, dst_ref=here, send_sem=send_sem.at[0], recv_sem=recv_sem.at[SLOT[name], j],
            device_id=place["S"], device_id_type=MESH,
        ).wait_recv()

    for c in (0, 1):

        @pl.when(logical == c)
        def _(c=c):
            send(c, (own, c), "S", "sib", 0, PIECES)
            for item in OWN[c]:
                where, target = item.split(".")
                name, j = target.split(":")
                send(c, (own, 1 if where == "P" else 0), where, name, int(j))

    multiplier, offset, cotangent = scalars[0], scalars[1], scalars[2]
    slope, shift = -multiplier, -offset

    def gradient(left, right):
        table = lax.dot_general(left, right, (((1,), (1,)), ((), ())), preferred_element_type=jnp.float32)
        return cotangent / (1.0 + jnp.exp(slope * table + shift))

    row = lax.broadcasted_iota(jnp.int32, (rows, rows), 0)
    paired = (row == match_ref[...]).astype(jnp.float32)
    turned = paired.T
    is_a = (kind == 0).astype(jnp.float32)
    positive = is_a * turned + (1.0 - is_a) * paired
    first = (gradient(own[1], own[0]) - cotangent * positive).astype(jnp.bfloat16)
    total[kind] = jnp.dot(first, own[0], preferred_element_type=jnp.float32)
    total[1 - kind] = lax.dot_general(first, own[1], (((0,), (0,)), ((), ())), preferred_element_type=jnp.float32)

    half = rows // 2

    def work(which, block, start, size):
        other = held[block, pl.ds(start, size)]
        grads = gradient(own[1 - which], other).astype(jnp.bfloat16)
        output = which * (1 - kind) + (1 - which) * kind
        total[output] += jnp.dot(grads, other, preferred_element_type=jnp.float32)

    arrived("sib", 0, PIECES)
    work(1 - logical, SLOT["sib"], 0, rows)

    steps = []
    for c in (0, 1):
        waited, list_c, events = set(), [], []
        for item in PLAN[c]:
            if ":" in item:
                name, j = item.split(":")
                events.append((name, int(j), FORWARD[c][name](int(j))))
                waited.add((name, int(j)))
                continue
            task = item.split(".")
            start = 0 if task[0] == "T" else 2 * int(task[2])
            for j in range(start, start + (PIECES if task[0] == "T" else 2)):
                if (task[1], j) not in waited:
                    assert task[1] not in FORWARD[c]
                    events.append((task[1], j, []))
                    waited.add((task[1], j))
            list_c.append((events, task[0] == "T", SLOT[task[1]], 0 if task[1][0] == "a" else 1, start))
            events = []
        missing = {(name, j) for name in NAMES for j in range(PIECES)} - waited
        assert not events and {name for name, _ in missing} == {"sib", "b4" if c == 0 else "a4"} - {n for n, _ in waited}
        steps.append(list_c)
    count = max(len(list_c) for list_c in steps)

    def lookup(k, field, default):
        values = []
        for list_c in steps:
            value = jnp.int32(default)
            for n in range(len(list_c)):
                value = jnp.where(k == n, int(list_c[n][field]), value)
            values.append(value)
        return jnp.where(logical == 0, values[0], values[1])

    def branch(k, low, high, run):
        if high - low == 1:
            run(low)
            return
        middle = (low + high) // 2

        @pl.when(k < middle)
        def _():
            branch(k, low, middle, run)

        @pl.when(k >= middle)
        def _():
            branch(k, middle, high, run)

    def take(c, n):
        for name, j, targets in steps[c][n][0]:
            arrived(name, j)
            for where, target in targets:
                send(c, (held, SLOT[name]), where, target, j)

    @pl.loop(0, count)
    def _(k):
        for c in (0, 1):

            @pl.when((logical == c) & (k < len(steps[c])))
            def _(c=c):
                branch(k, 0, len(steps[c]), functools.partial(take, c))

        full = lookup(k, 1, 2)
        block = lookup(k, 2, 0)
        which = lookup(k, 3, 0)
        start = lookup(k, 4, 0) * part

        @pl.when(full == 1)
        def _():
            work(which, block, 0, rows)

        @pl.when(full == 0)
        def _():
            work(which, block, pl.multiple_of(start, half), half)

    for c in (0, 1):

        @pl.when(logical == c)
        def _(c=c):
            for copy in sent[c]:
                copy().wait_send()


def per_device(pictures, captions, matched, multiplier, offset, cotangent):
    rows, width = pictures.shape
    scalars = jnp.stack([multiplier, offset, cotangent])
    matched, pictures, captions = (pltpu.with_memory_space_constraint(v, pltpu.HBM) for v in (matched, pictures, captions))
    sums = pl.pallas_call(
        functools.partial(kernel, rows),
        out_shape=jax.ShapeDtypeStruct((2, rows, width), jnp.float32),
        in_specs=[
            pl.BlockSpec(memory_space=pltpu.SMEM),
            pl.BlockSpec(memory_space=pltpu.HBM),
            pl.BlockSpec(memory_space=pltpu.HBM),
            pl.BlockSpec(memory_space=pltpu.HBM),
        ],
        out_specs=pl.BlockSpec(memory_space=pltpu.VMEM),
        scratch_shapes=[
            pltpu.VMEM((2, rows, width), jnp.bfloat16),
            pltpu.VMEM((len(NAMES), rows, width), jnp.bfloat16),
            pltpu.VMEM((1, rows), jnp.int32),
            pltpu.SemaphoreType.DMA((3,)),
            pltpu.SemaphoreType.DMA((80,)),
            pltpu.SemaphoreType.DMA((len(NAMES), PIECES)),
        ],
        compiler_params=pltpu.CompilerParams(
            collective_id=0, has_side_effects=True, vmem_limit_bytes=LIMIT * 2**20
        ),
        cost_estimate=pl.CostEstimate(
            flops=31 * 2 * rows * rows * width, bytes_accessed=12 * rows * width, transcendentals=16 * rows * rows
        ),
        name="band",
    )(scalars, matched, pictures, captions)
    return multiplier * sums[0], multiplier * sums[1]


def solution(mesh):
    placed = (P("dp", None), P("dp", None), P("dp", None), P(), P(), P())
    return jax.shard_map(
        per_device,
        mesh=mesh,
        in_specs=placed,
        out_specs=(P("dp", None), P("dp", None)),
        check_vma=False,
    )
```

time: 88.6 us -> 73.7 us (0.83)
  Pallas kernels: 79 us -> 68.5 us
  local copies, waits for them, and re-layouts: 6.74 us -> 0 us
  other arithmetic: 0.08 us -> 2.56 us
    pallas_call x1, Pallas kernels: 79 us -> 68.5 us  [per_device(): pl.pallas_call(functools.partial(kernel, rows), out_shape=jax.ShapeDtypeS...]
    unnamed x8 -> x0, local copies, waits for them, and re-layouts: 6.74 us -> none
    mul x0 -> x1, other arithmetic: none -> 2.49 us  [per_device(): return (multiplier * sums[0], multiplier * sums[1])]
where the time goes in v2:
time: 73.7 us; the launch traced here: 73.6 us
  Pallas kernels  68.5 us (93%)
  between operations  2.58 us (4%)
  other arithmetic  2.56 us (3%)
    pallas_call x1, Pallas kernels, per_device(): pl.pallas_call(functools.partial(kernel, rows), out_shape=jax.ShapeDtypeS...  68.5 us
    mul x1, other arithmetic, per_device(): return (multiplier * sums[0], multiplier * sums[1])  2.49 us

profile of v2, /device:TPU:1, one launch (start us, length us, event | category | flops | bytes accessed | tf_op | source)
XLA Modules:
  0.0 73.6 jit_solution(7433682237277187370)
XLA Ops:
  2.6 0.1 pad_maximum_fusion.scalars
  2.6 68.5 %band.1 = f32[2,512,1152]{2,1,0:T(8,128)S(1)} custom-call(f32[3]{0:T(128)S(1)} %pad_maximum_fusion.scalars, s32[1,512]{1,0:T(1,128)} %match_hbm.1, bf16[512,1152]{1,0:T(8,128)(2,1)} %picture_hbm.1, bf16[512,1152]{1,0:T(8,128)(2,1)} %caption_hbm.1), custom_call_target="tpu_custom_call" | custom-call | flops 18723373056 | bytes 7077888 | tf_op jit(solution)/shard_map/band/pallas_call | solution.py:301
  71.1 2.5 %multiply_bitcast_fusion = (f32[512,1152]{1,0:T(8,128)}, f32[512,1152]{1,0:T(8,128)}) fusion(f32[2,512,1152]{2,1,0:T(8,128)S(1)} %band.1, f32[]{:T(128)} %copy.8), kind=kLoop, calls=%fused_computation | loop fusion | flops 1179648 | bytes 9437188 | tf_op jit(solution)/shard_map/mul | solution.py:327

commit v3 on v2

--- a/solution.py
+++ b/solution.py
@@ -8,8 +8,8 @@
 from jax.sharding import PartitionSpec as P
 
 MESH = pl.DeviceIdType.MESH
-PIECES = 4
-SPLIT = 3
+PIECES = 8
+SPLIT = 5
 LIMIT = 36
 
 NAMES = (
@@ -38,55 +38,63 @@
     },
 )
 
+sib, b1_0, b1_1, a2_0, a2_1, b2_0, b2_1, a1_0, a1_1, b3_0, b3_1, a3_0, a3_1, a4, b4 = NAMES
+T, H, D, SEND, N, P_, X = "T", "H", "D", ">", "N", "P", "X"
+
 OWN = (
     [
-        "P.b2_0:0", "X.b1_1:3", "P.b2_0:1", "X.b1_1:0", "N.a2_0:1", "P.b2_0:2", "N.a2_0:2", "X.b1_1:2",
-        "N.a2_0:0", "X.b1_1:1", "P.b2_0:3",
+        (N, a2_0, 0), (X, b1_1, 4), (X, b1_1, 6), (X, b1_1, 7), (P_, b2_0, 0), (P_, b2_0, 3), (X, b1_1, 1),
+        (X, b1_1, 3), (N, a2_0, 2),
     ],
     [
-        "N.a2_1:2", "P.b2_1:3", "X.b1_0:0", "P.b2_1:2", "P.b2_1:0", "N.a2_1:3", "P.b2_1:1", "X.b1_0:3",
-        "N.a2_1:1", "X.b1_0:2", "X.b1_0:1", "N.a2_1:0",
+        (P_, b2_1, 3), (X, b1_0, 6), (P_, b2_1, 4), (N, a2_1, 4),
     ],
 )
 
 PLAN = (
     [
-        "b2_0:0", "a2_0:1", "a2_0:2", "b2_0:1", "H.b1_1.1",
-        "H.b1_1.0",
-        "b2_0:2", "a2_0:0", "a1_0:3", "b1_0:3", "b1_0:1", "b1_0:0", "b1_0:2", "T.b1_0",
-        "b2_0:3", "H.a2_0.0",
-        "b3_0:2", "H.b2_1.1",
-        "H.a2_1.1",
-        "b3_0:3", "H.b3_0.1",
-        "H.a2_1.0",
-        "a1_0:2", "T.b2_0",
-        "b3_0:1", "b4:0", "T.b3_1",
-        "b4:1", "a1_0:1", "a1_0:0", "H.b2_1.0",
-        "b4:2", "T.a1_0",
-        "a3_0:3", "a2_0:3", "a3_0:2", "b4:3", "b3_0:0", "T.a1_1",
-        "T.a4",
-        "H.b3_0.0",
-        "H.a2_0.1",
-        "a3_0:1", "a3_0:0", "T.a3_0",
-        "T.a3_1",
+        (SEND, P_, b2_0, 4), (SEND, X, b1_1, 2), (SEND, X, b1_1, 0), (SEND, X, b1_1, 5), (SEND, P_, b2_0, 5),
+        (SEND, N, a2_0, 4), (SEND, N, a2_0, 1), (SEND, P_, b2_0, 6), (b1_0, 0), (a2_0, 0), (SEND, P_, b2_0, 1),
+        (b1_0, 6), (SEND, N, a2_0, 3), (SEND, P_, b2_0, 7), (a2_0, 1), (b1_0, 4), (a1_0, 3), (SEND, P_, b2_0, 2),
+        (T, b1_1),
+        (b1_0, 5), (b1_0, 7), (H, b1_0, 1),
+        (b3_0, 6), (b1_0, 3), (a2_0, 2), (b3_0, 0), (a1_0, 1), (H, a2_1, 0),
+        (a2_0, 4), (b1_0, 2), (a1_0, 4), (b2_0, 4), (b2_0, 0), (b2_0, 1), (b2_0, 2), (b2_0, 3),
+        (D, a2_1, 1, b2_0, 0),
+        (b2_0, 5), (b2_0, 6), (b2_0, 7), (H, b2_0, 1),
+        (b3_0, 1), (b3_0, 2), (b3_0, 3), (b3_0, 4), (b3_0, 5), (b3_0, 7), (T, b3_0),
+        (b1_0, 1), (a2_0, 3), (T, b2_1),
+        (a1_0, 2), (a1_0, 0), (b4, 0), (H, b1_0, 0),
+        (a1_0, 5), (a1_0, 6), (a1_0, 7), (T, a1_0),
+        (H, b3_1, 1),
+        (b4, 1), (H, b3_1, 0),
+        (b4, 2), (b4, 5), (b4, 3), (a2_0, 7), (b4, 4), (a2_0, 6), (a3_0, 1), (a2_0, 5), (T, a2_0),
+        (a3_0, 4), (b4, 6), (a3_0, 0), (b4, 7), (a3_0, 2), (T, a1_1),
+        (a3_0, 5), (a3_0, 3), (D, a4, 1, a3_0, 0),
+        (a3_0, 6), (a3_0, 7), (D, a4, 0, a3_0, 1),
+        (T, a3_1),
     ],
     [
-        "b1_1:0", "b1_1:3", "b1_1:2", "b2_1:3", "a1_1:0", "b1_1:1", "a2_1:2", "H.b1_1.0",
-        "a2_1:3", "H.a2_0.0",
-        "b3_1:2", "b3_1:1", "a2_1:1", "H.b1_1.1",
-        "b2_1:1", "b2_1:2", "a2_1:0", "T.a2_1",
-        "b2_1:0", "T.b2_0",
-        "b3_1:0", "b3_1:3", "T.b3_1",
-        "a1_1:3", "T.b2_1",
-        "T.b1_0",
-        "a1_1:1", "H.a1_1.0",
-        "a1_1:2", "H.a1_1.1",
-        "T.a1_0",
-        "H.a2_0.1",
-        "T.b4",
-        "a3_1:0", "T.b3_0",
-        "a3_1:2", "a3_1:1", "a3_1:3", "T.a3_1",
-        "T.a3_0",
+        (SEND, X, b1_0, 0), (SEND, X, b1_0, 7), (SEND, P_, b2_1, 5), (SEND, N, a2_1, 3), (SEND, X, b1_0, 4),
+        (SEND, X, b1_0, 1), (b1_1, 3), (SEND, N, a2_1, 1), (SEND, P_, b2_1, 2), (SEND, N, a2_1, 6),
+        (SEND, X, b1_0, 3), (SEND, N, a2_1, 0), (SEND, N, a2_1, 5), (SEND, P_, b2_1, 1), (b1_1, 4),
+        (SEND, X, b1_0, 2), (SEND, P_, b2_1, 6), (SEND, X, b1_0, 5), (SEND, P_, b2_1, 0), (b2_1, 5), (b1_1, 6),
+        (b2_1, 2), (SEND, P_, b2_1, 7), (b1_1, 0), (b1_1, 5), (SEND, N, a2_1, 2), (b2_1, 4), (SEND, N, a2_1, 7),
+        (b1_1, 7), (b2_1, 3), (a2_1, 6), (b1_1, 1), (b1_1, 2), (H, b1_1, 0),
+        (H, b1_1, 1),
+        (b2_1, 1), (a2_1, 1), (a2_1, 0), (a2_1, 2), (a2_1, 3), (a2_1, 4), (a2_1, 5), (a2_1, 7), (T, a2_1),
+        (b2_1, 0), (b2_1, 6), (b2_1, 7), (T, b2_1),
+        (T, b2_0),
+        (H, b1_0, 0),
+        (H, b1_0, 1),
+        (a1_1, 0), (b3_1, 6), (b3_1, 4), (b3_1, 2), (b3_1, 5), (b3_1, 7), (D, b3_1, 1, b3_0, 0),
+        (a1_1, 3), (b3_1, 0), (b3_1, 1), (b3_1, 3), (D, b3_1, 0, b3_0, 1),
+        (a1_1, 1), (a1_1, 2), (a1_1, 4), (a1_1, 5), (a1_1, 6), (a1_1, 7), (T, a1_1),
+        (T, a1_0),
+        (T, a2_0),
+        (T, b4),
+        (a3_1, 2), (a3_1, 6), (a3_1, 5), (a3_1, 0), (a3_1, 1), (a3_1, 3), (a3_1, 4), (a3_1, 7), (T, a3_1),
+        (T, a3_0),
     ],
 )
 
@@ -176,15 +184,17 @@
             device_id=place["S"], device_id_type=MESH,
         ).wait_recv()
 
+    def send_own(c, item):
+        where, name, j = item
+        send(c, (own, 1 if where == "P" else 0), where, name, j)
+
     for c in (0, 1):
 
         @pl.when(logical == c)
         def _(c=c):
             send(c, (own, c), "S", "sib", 0, PIECES)
             for item in OWN[c]:
-                where, target = item.split(".")
-                name, j = target.split(":")
-                send(c, (own, 1 if where == "P" else 0), where, name, int(j))
+                send_own(c, item)
 
     multiplier, offset, cotangent = scalars[0], scalars[1], scalars[2]
     slope, shift = -multiplier, -offset
@@ -217,19 +227,27 @@
     for c in (0, 1):
         waited, list_c, events = set(), [], []
         for item in PLAN[c]:
-            if ":" in item:
-                name, j = item.split(":")
-                events.append((name, int(j), FORWARD[c][name](int(j))))
-                waited.add((name, int(j)))
+            if item[0] == SEND:
+                events.append((item[1:], None, []))
                 continue
-            task = item.split(".")
-            start = 0 if task[0] == "T" else 2 * int(task[2])
-            for j in range(start, start + (PIECES if task[0] == "T" else 2)):
-                if (task[1], j) not in waited:
-                    assert task[1] not in FORWARD[c]
-                    events.append((task[1], j, []))
-                    waited.add((task[1], j))
-            list_c.append((events, task[0] == "T", SLOT[task[1]], 0 if task[1][0] == "a" else 1, start))
+            if item[0] not in (T, H, D):
+                name, j = item
+                events.append((name, j, FORWARD[c][name](j)))
+                waited.add((name, j))
+                continue
+            halves = [(item[1], 0), (item[1], 1)] if item[0] == T else []
+            for n in range(1, len(item) - 1, 2):
+                halves.append((item[n], item[n + 1]))
+            for name, h in halves:
+                for j in range(h * PIECES // 2, (h + 1) * PIECES // 2):
+                    if (name, j) not in waited:
+                        assert name not in FORWARD[c]
+                        events.append((name, j, []))
+                        waited.add((name, j))
+            fields = [events, (H, T, D).index(item[0])]
+            for name, h in (halves[0], halves[-1]):
+                fields += [SLOT[name], 0 if name[0] == "a" else 1, h]
+            list_c.append(fields)
             events = []
         missing = {(name, j) for name in NAMES for j in range(PIECES)} - waited
         assert not events and {name for name, _ in missing} == {"sib", "b4" if c == 0 else "a4"} - {n for n, _ in waited}
@@ -261,6 +279,9 @@
 
     def take(c, n):
         for name, j, targets in steps[c][n][0]:
+            if j is None:
+                send_own(c, name)
+                continue
             arrived(name, j)
             for where, target in targets:
                 send(c, (held, SLOT[name]), where, target, j)
@@ -273,18 +294,27 @@
             def _(c=c):
                 branch(k, 0, len(steps[c]), functools.partial(take, c))
 
-        full = lookup(k, 1, 2)
-        block = lookup(k, 2, 0)
-        which = lookup(k, 3, 0)
-        start = lookup(k, 4, 0) * part
-
-        @pl.when(full == 1)
+        form = lookup(k, 1, 3)
+        block, which, start = lookup(k, 2, 0), lookup(k, 3, 0), lookup(k, 4, 0) * half
+
+        @pl.when(form == 1)
         def _():
             work(which, block, 0, rows)
 
-        @pl.when(full == 0)
+        @pl.when(form == 0)
         def _():
             work(which, block, pl.multiple_of(start, half), half)
+
+        @pl.when(form == 2)
+        def _():
+            second = lookup(k, 5, 0), lookup(k, 6, 0), lookup(k, 7, 0) * half
+            pair = []
+            for block_, which_, start_ in ((block, which, start), second):
+                other = held[block_, pl.ds(pl.multiple_of(start_, half), half)]
+                pair.append((which_, other, gradient(own[1 - which_], other).astype(jnp.bfloat16)))
+            for which_, other, grads in pair:
+                output = which_ * (1 - kind) + (1 - which_) * kind
+                total[output] += jnp.dot(grads, other, preferred_element_type=jnp.float32)
 
     for c in (0, 1):
 
@@ -313,7 +343,7 @@
             pltpu.VMEM((len(NAMES), rows, width), jnp.bfloat16),
             pltpu.VMEM((1, rows), jnp.int32),
             pltpu.SemaphoreType.DMA((3,)),
-            pltpu.SemaphoreType.DMA((80,)),
+            pltpu.SemaphoreType.DMA((160,)),
             pltpu.SemaphoreType.DMA((len(NAMES), PIECES)),
         ],
         compiler_params=pltpu.CompilerParams(

time: 73.7 us -> 73.3 us (level)
  no operation moved by 1% of the time
where the time goes in v3:
time: 73.3 us; the launch traced here: 73.2 us
  Pallas kernels  68 us (93%)
  between operations  2.58 us (4%)
  other arithmetic  2.56 us (3%)
    pallas_call x1, Pallas kernels, per_device(): pl.pallas_call(functools.partial(kernel, rows), out_shape=jax.ShapeDtypeS...  68 us
    mul x1, other arithmetic, per_device(): return (multiplier * sums[0], multiplier * sums[1])  2.49 us

profile of v3, /device:TPU:1, one launch (start us, length us, event | category | flops | bytes accessed | tf_op | source)
XLA Modules:
  0.0 73.2 jit_solution(18013478641586648847)
XLA Ops:
  2.6 0.1 pad_maximum_fusion.scalars
  2.6 68.0 %band.1 = f32[2,512,1152]{2,1,0:T(8,128)S(1)} custom-call(f32[3]{0:T(128)S(1)} %pad_maximum_fusion.scalars, s32[1,512]{1,0:T(1,128)} %match_hbm.1, bf16[512,1152]{1,0:T(8,128)(2,1)} %picture_hbm.1, bf16[512,1152]{1,0:T(8,128)(2,1)} %caption_hbm.1), custom_call_target="tpu_custom_call" | custom-call | flops 18723373056 | bytes 7077888 | tf_op jit(solution)/shard_map/band/pallas_call | solution.py:331
  70.7 2.5 %multiply_bitcast_fusion = (f32[512,1152]{1,0:T(8,128)}, f32[512,1152]{1,0:T(8,128)}) fusion(f32[2,512,1152]{2,1,0:T(8,128)S(1)} %band.1, f32[]{:T(128)} %copy.8), kind=kLoop, calls=%fused_computation | loop fusion | flops 1179648 | bytes 9437188 | tf_op jit(solution)/shard_map/mul | solution.py:357

commit v4 on v3

--- a/solution.py
+++ b/solution.py
@@ -43,36 +43,27 @@
 
 OWN = (
     [
-        (N, a2_0, 0), (X, b1_1, 4), (X, b1_1, 6), (X, b1_1, 7), (P_, b2_0, 0), (P_, b2_0, 3), (X, b1_1, 1),
-        (X, b1_1, 3), (N, a2_0, 2),
+        (N, a2_0, 0), (X, b1_1, 4), (X, b1_1, 6), (P_, b2_0, 0), (X, b1_1, 7), (X, b1_1, 1), (X, b1_1, 3),
+        (N, a2_0, 2), (P_, b2_0, 6),
     ],
     [
-        (P_, b2_1, 3), (X, b1_0, 6), (P_, b2_1, 4), (N, a2_1, 4),
+        (P_, b2_1, 3), (N, a2_1, 4), (X, b1_0, 6), (P_, b2_1, 4),
     ],
 )
 
 PLAN = (
     [
-        (SEND, P_, b2_0, 4), (SEND, X, b1_1, 2), (SEND, X, b1_1, 0), (SEND, X, b1_1, 5), (SEND, P_, b2_0, 5),
-        (SEND, N, a2_0, 4), (SEND, N, a2_0, 1), (SEND, P_, b2_0, 6), (b1_0, 0), (a2_0, 0), (SEND, P_, b2_0, 1),
-        (b1_0, 6), (SEND, N, a2_0, 3), (SEND, P_, b2_0, 7), (a2_0, 1), (b1_0, 4), (a1_0, 3), (SEND, P_, b2_0, 2),
-        (T, b1_1),
-        (b1_0, 5), (b1_0, 7), (H, b1_0, 1),
-        (b3_0, 6), (b1_0, 3), (a2_0, 2), (b3_0, 0), (a1_0, 1), (H, a2_1, 0),
-        (a2_0, 4), (b1_0, 2), (a1_0, 4), (b2_0, 4), (b2_0, 0), (b2_0, 1), (b2_0, 2), (b2_0, 3),
-        (D, a2_1, 1, b2_0, 0),
-        (b2_0, 5), (b2_0, 6), (b2_0, 7), (H, b2_0, 1),
-        (b3_0, 1), (b3_0, 2), (b3_0, 3), (b3_0, 4), (b3_0, 5), (b3_0, 7), (T, b3_0),
-        (b1_0, 1), (a2_0, 3), (T, b2_1),
-        (a1_0, 2), (a1_0, 0), (b4, 0), (H, b1_0, 0),
-        (a1_0, 5), (a1_0, 6), (a1_0, 7), (T, a1_0),
-        (H, b3_1, 1),
-        (b4, 1), (H, b3_1, 0),
-        (b4, 2), (b4, 5), (b4, 3), (a2_0, 7), (b4, 4), (a2_0, 6), (a3_0, 1), (a2_0, 5), (T, a2_0),
-        (a3_0, 4), (b4, 6), (a3_0, 0), (b4, 7), (a3_0, 2), (T, a1_1),
-        (a3_0, 5), (a3_0, 3), (D, a4, 1, a3_0, 0),
-        (a3_0, 6), (a3_0, 7), (D, a4, 0, a3_0, 1),
-        (T, a3_1),
+        (SEND, P_, b2_0, 4), (SEND, X, b1_1, 2), (SEND, N, a2_0, 4), (SEND, P_, b2_0, 3), (SEND, X, b1_1, 0),
+        (SEND, X, b1_1, 5), (SEND, P_, b2_0, 5), (SEND, N, a2_0, 1), (b1_0, 0), (a2_0, 0), (SEND, P_, b2_0, 1),
+        (b1_0, 6), (SEND, N, a2_0, 3), (SEND, P_, b2_0, 7), (a2_0, 1), (b1_0, 4), (a1_0, 3),
+        (SEND, P_, b2_0, 2), (T, b1_1), (b1_0, 5), (b1_0, 7), (H, b1_0, 1), (b3_0, 6), (b1_0, 3), (a2_0, 2),
+        (b3_0, 0), (a1_0, 1), (H, a2_1, 0), (a2_0, 4), (b1_0, 2), (a1_0, 4), (b2_0, 4), (b2_0, 0), (b2_0, 1),
+        (b2_0, 2), (b2_0, 3), (D, a2_1, 1, b2_0, 0), (b2_0, 5), (b2_0, 6), (b2_0, 7), (H, b2_0, 1), (b3_0, 1),
+        (b3_0, 2), (b3_0, 3), (b3_0, 4), (b3_0, 5), (b3_0, 7), (T, b3_0), (b1_0, 1), (a2_0, 3), (T, b2_1),
+        (a1_0, 0), (b4, 0), (H, b1_0, 0), (a1_0, 2), (a1_0, 5), (a1_0, 6), (a1_0, 7), (T, a1_0), (H, b3_1, 1),
+        (b4, 1), (H, b3_1, 0), (b4, 2), (b4, 5), (b4, 3), (a2_0, 7), (b4, 4), (a2_0, 6), (a3_0, 1), (a2_0, 5),
+        (T, a2_0), (a3_0, 4), (b4, 6), (a3_0, 0), (b4, 7), (a3_0, 2), (T, a1_1), (a3_0, 5), (a3_0, 3),
+        (D, a4, 1, a3_0, 0), (a3_0, 6), (a3_0, 7), (D, a4, 0, a3_0, 1), (T, a3_1),
     ],
     [
         (SEND, X, b1_0, 0), (SEND, X, b1_0, 7), (SEND, P_, b2_1, 5), (SEND, N, a2_1, 3), (SEND, X, b1_0, 4),
@@ -80,21 +71,13 @@
         (SEND, X, b1_0, 3), (SEND, N, a2_1, 0), (SEND, N, a2_1, 5), (SEND, P_, b2_1, 1), (b1_1, 4),
         (SEND, X, b1_0, 2), (SEND, P_, b2_1, 6), (SEND, X, b1_0, 5), (SEND, P_, b2_1, 0), (b2_1, 5), (b1_1, 6),
         (b2_1, 2), (SEND, P_, b2_1, 7), (b1_1, 0), (b1_1, 5), (SEND, N, a2_1, 2), (b2_1, 4), (SEND, N, a2_1, 7),
-        (b1_1, 7), (b2_1, 3), (a2_1, 6), (b1_1, 1), (b1_1, 2), (H, b1_1, 0),
-        (H, b1_1, 1),
-        (b2_1, 1), (a2_1, 1), (a2_1, 0), (a2_1, 2), (a2_1, 3), (a2_1, 4), (a2_1, 5), (a2_1, 7), (T, a2_1),
-        (b2_1, 0), (b2_1, 6), (b2_1, 7), (T, b2_1),
-        (T, b2_0),
-        (H, b1_0, 0),
-        (H, b1_0, 1),
-        (a1_1, 0), (b3_1, 6), (b3_1, 4), (b3_1, 2), (b3_1, 5), (b3_1, 7), (D, b3_1, 1, b3_0, 0),
-        (a1_1, 3), (b3_1, 0), (b3_1, 1), (b3_1, 3), (D, b3_1, 0, b3_0, 1),
-        (a1_1, 1), (a1_1, 2), (a1_1, 4), (a1_1, 5), (a1_1, 6), (a1_1, 7), (T, a1_1),
-        (T, a1_0),
-        (T, a2_0),
-        (T, b4),
-        (a3_1, 2), (a3_1, 6), (a3_1, 5), (a3_1, 0), (a3_1, 1), (a3_1, 3), (a3_1, 4), (a3_1, 7), (T, a3_1),
-        (T, a3_0),
+        (b1_1, 7), (b2_1, 3), (a2_1, 6), (b1_1, 1), (b1_1, 2), (T, b1_1), (b2_1, 1), (a2_1, 1), (a2_1, 0),
+        (a2_1, 2), (a2_1, 3), (a2_1, 4), (a2_1, 5), (a2_1, 7), (T, a2_1), (b2_1, 0), (b2_1, 6), (b2_1, 7),
+        (T, b2_1), (T, b2_0), (H, b1_0, 0), (H, b1_0, 1), (a1_1, 0), (b3_1, 6), (b3_1, 4), (b3_1, 2), (b3_1, 5),
+        (b3_1, 7), (D, b3_1, 1, b3_0, 0), (a1_1, 3), (b3_1, 0), (b3_1, 1), (b3_1, 3), (D, b3_1, 0, b3_0, 1),
+        (a1_1, 1), (a1_1, 2), (a1_1, 4), (a1_1, 5), (a1_1, 6), (a1_1, 7), (T, a1_1), (T, a1_0), (T, a2_0),
+        (T, b4), (a3_1, 2), (a3_1, 6), (a3_1, 5), (a3_1, 0), (a3_1, 1), (a3_1, 3), (a3_1, 4), (a3_1, 7),
+        (T, a3_1), (T, a3_0),
     ],
 )
 

time: 73.3 us -> 73.3 us (level)
  no operation moved by 1% of the time
where the time goes in v4:
time: 73.3 us; the launch traced here: 73.2 us
  Pallas kernels  68 us (93%)
  between operations  2.58 us (4%)
  other arithmetic  2.56 us (3%)
    pallas_call x1, Pallas kernels, per_device(): pl.pallas_call(functools.partial(kernel, rows), out_shape=jax.ShapeDtypeS...  68 us
    mul x1, other arithmetic, per_device(): return (multiplier * sums[0], multiplier * sums[1])  2.49 us

profile of v4, /device:TPU:1, one launch (start us, length us, event | category | flops | bytes accessed | tf_op | source)
XLA Modules:
  0.0 73.2 jit_solution(8945119181158380800)
XLA Ops:
  2.6 0.1 pad_maximum_fusion.scalars
  2.6 68.0 %band.1 = f32[2,512,1152]{2,1,0:T(8,128)S(1)} custom-call(f32[3]{0:T(128)S(1)} %pad_maximum_fusion.scalars, s32[1,512]{1,0:T(1,128)} %match_hbm.1, bf16[512,1152]{1,0:T(8,128)(2,1)} %picture_hbm.1, bf16[512,1152]{1,0:T(8,128)(2,1)} %caption_hbm.1), custom_call_target="tpu_custom_call" | custom-call | flops 18723373056 | bytes 7077888 | tf_op jit(solution)/shard_map/band/pallas_call | solution.py:314
  70.7 2.5 %multiply_bitcast_fusion = (f32[512,1152]{1,0:T(8,128)}, f32[512,1152]{1,0:T(8,128)}) fusion(f32[2,512,1152]{2,1,0:T(8,128)S(1)} %band.1, f32[]{:T(128)} %copy.8), kind=kLoop, calls=%fused_computation | loop fusion | flops 1179648 | bytes 9437188 | tf_op jit(solution)/shard_map/mul | solution.py:340
